TPU v7x, 512 devices: a whole 4x4x16 slice. The times are simulated.
512 devices in a mesh: tm: 64 (over z, x_hi, core), mic: 8 (over x_lo, y).
Axes of the slice: x: 4 (x_hi: 2, x_lo: 2; x = x_hi * 2 + x_lo), y: 4, z: 16, core: 2. Of those that a mesh axis runs over, the one named last changes fastest.
Arguments:
- signal: bfloat16 [262144, 4096], P('tm', 'mic')
- mic_pos: int32 [3, 4096], P(None, 'mic'), may hold values from 0 to 255, as said below
- grid_pos: int32 [3, 8192], replicated, may hold values from 0 to 255, as said below
- bins: int32 [2], replicated, may hold values from 1 to 511, as said below
Outputs:
- power: float32 [8192], P('mic')
Inputs may be any that keep to these rules, and one draw needn't show every extreme that they name: `mic_pos`: rows are x, y, z; a microphone's z is below 16. `grid_pos`: rows are x, y, z; a grid point's z is 64 or more and below 128. `bins`: the bin indices are distinct; the first is 511.
All inputs are finite; a program needn't handle non-finite values.
Results may differ from a plain program's by a relative error of at most 0.0006.
The roundings to bfloat16 on the way count: a program that leaves them out, or rounds other values in their place, can miss the bound.
Values may be sent and summed in bfloat16 or wider, within the bound.
A program may use at most 64 MiB of HBM per device.

v0:
```python
import math
import jax
import jax.numpy as jnp
from jax import lax
from jax.sharding import PartitionSpec as P

MICS = 4096
SEGLEN = 8192
NBINS = 2


def from_behind(shard, axis, by):
    size = lax.axis_size(axis)
    pairs = [(i, i + by) for i in range(size) if 0 <= i + by < size]
    return lax.ppermute(shard, axis, pairs)


def fourier_rows(bins):
    sample_index = jnp.arange(SEGLEN, dtype=jnp.int32)
    window = 0.5 - 0.5 * jnp.cos(2.0 * math.pi * sample_index.astype(jnp.float32) / SEGLEN)
    phases = bins[:, None] * sample_index[None, :] % SEGLEN
    angles = 2.0 * math.pi * phases.astype(jnp.float32) / SEGLEN
    weighting = window / math.sqrt(0.375 * SEGLEN)
    fourier = jnp.stack([weighting * jnp.cos(angles), -weighting * jnp.sin(angles)], axis=1)
    return fourier.reshape(2 * NBINS, SEGLEN).astype(jnp.bfloat16)


def steer_block(points, mic_pos, bins):
    offsets = points[:, :, None] - mic_pos[:, None, :]
    distance = jnp.sqrt(jnp.sum(offsets * offsets, axis=0).astype(jnp.float32))
    strength = 16.0 / distance
    cycles = bins.astype(jnp.float32)[:, None, None] * distance[None] * (16.0 / SEGLEN)
    cosine_part = (strength[None] * jnp.cos(2.0 * math.pi * cycles)).astype(jnp.bfloat16)
    sine_part = (strength[None] * jnp.sin(2.0 * math.pi * cycles)).astype(jnp.bfloat16)
    return (cosine_part, sine_part)


def steered(spectra, cosine_part, sine_part):
    segments = spectra.shape[0]
    mic_count = spectra.shape[2]
    width = cosine_part.shape[1]
    per_bin = []
    for bin_index in range(NBINS):
        bin_pair = spectra[:, 2 * bin_index : 2 * bin_index + 2, :].reshape(2 * segments, mic_count)
        cosine_sum = jnp.dot(
            bin_pair, cosine_part[bin_index].T, preferred_element_type=jnp.float32
        ).reshape(segments, 2, width)
        sine_sum = jnp.dot(
            bin_pair, sine_part[bin_index].T, preferred_element_type=jnp.float32
        ).reshape(segments, 2, width)
        real_part = cosine_sum[:, 0] - sine_sum[:, 1]
        imag_part = cosine_sum[:, 1] + sine_sum[:, 0]
        per_bin.append(jnp.stack([real_part, imag_part], axis=1))
    return jnp.stack(per_bin, axis=1)


def beams_for(spectra, chosen_points, mic_pos, bins):
    point_count = chosen_points.shape[1]
    block_width = min(point_count, 1024)
    block_count = point_count // block_width
    points = chosen_points.reshape(3, block_count, block_width).transpose(1, 0, 2)

    def block_beam(block_points):
        cosine_part, sine_part = steer_block(block_points, mic_pos, bins)
        return steered(spectra, cosine_part, sine_part)

    partial_value = lax.map(block_beam, points)
    segments = spectra.shape[0]
    return partial_value.transpose(1, 2, 3, 0, 4).reshape(segments, NBINS, 2, point_count)


def local(signal, mic_pos, grid_pos, bins):
    fourier = fourier_rows(bins)
    following = from_behind(signal, "tm", -1)
    segment = jnp.concatenate([signal, following], axis=0)
    spectrum = jnp.dot(fourier, segment, preferred_element_type=jnp.float32)
    spectrum = spectrum.astype(jnp.bfloat16)
    grid_count = grid_pos.shape[1]
    owners = lax.axis_size("mic")
    owned_count = grid_count // owners
    spans = lax.axis_size("tm")
    partial_value = beams_for(spectrum[None], grid_pos, mic_pos, bins)[0]
    summed = lax.psum(partial_value, "mic")
    owned = lax.dynamic_slice_in_dim(summed, lax.axis_index("mic") * owned_count, owned_count, 2)
    local_power = jnp.sum(owned * owned, axis=(0, 1))
    power_sum = lax.psum(local_power, "tm")
    return power_sum / (spans * NBINS * MICS)


def solution(mesh):
    in_specs = (P("tm", "mic"), P(None, "mic"), P(), P())
    out_specs = P("mic")
    return jax.shard_map(local, mesh=mesh, in_specs=in_specs, out_specs=out_specs, check_vma=False)
```

profile of v0, /device:TPU:1, one launch (start us, length us, event | category | flops | bytes accessed | tf_op | source)
XLA Modules:
  0.0 457.2 jit_solution(10412396298532731741)
XLA Ops:
  6.5 8.8 %collective-permute-start = (bf16[4096,512]{1,0:T(8,128)(2,1)}, bf16[4096,512]{1,0:T(8,128)(2,1)}, u32[]{:S(2)}, u32[]{:S(2)}) collective-permute-start(bf16[4096,512]{1,0:T(8,128)(2,1)} %param.6), channel_id=1, source_target_pairs={{8,0},{16,8},{24,16},{32,24},{40,32},{48,40},{56,48},{64,56},{72,6... | collective-permute-start | bytes 12582920 | tf_op jit(solution)/shard_map/ppermute | solution.py:15
  15.5 1.9 multiply_convert_fusion.3
  17.6 0.7 convert_bitcast_fusion
  18.3 40.8 %collective-permute-done = bf16[4096,512]{1,0:T(8,128)(2,1)} collective-permute-done((bf16[4096,512]{1,0:T(8,128)(2,1)}, bf16[4096,512]{1,0:T(8,128)(2,1)}, u32[]{:S(2)}, u32[]{:S(2)}) %collective-permute-start) | collective-permute-done | bytes 4194336 | tf_op jit(solution)/shard_map/ppermute | solution.py:15
  59.1 4.6 %fusion.16 = bf16[1,4,512]{2,1,0:T(4,128)(2,1)S(1)} fusion(bf16[4,8192]{1,0:T(4,128)(2,1)S(1)} %convert_element_type.74, bf16[4096,512]{1,0:T(8,128)(2,1)} %collective-permute-done, bf16[4096,512]{1,0:T(8,128)(2,1)} %param.6), kind=kOutput, calls=%fused_computation.36 | convolution fusion | flops 50333696 | bytes 8458240 | tf_op jit(solution)/shard_map/dot_general | solution.py:76
  63.7 161.1 %while.12 = (s32[]{:T(128)}, f32[8,1,2,2,1024]{4,3,2,1,0:T(2,128)S(1)}, s32[8,3,1024]{2,1,0:T(4,128)}, s32[3,512]{1,0:T(4,128)S(1)}, f32[2,1,1]{0,2,1:T(1,128)S(1)}, /*index=5*/bf16[1,4,512]{2,1,0:T(4,128)(2,1)S(1)}, s32[]{:T(128)}) while((s32[]{:T(128)}, f32[8,1,2,2,1024]{4,3,2,1,0:T(2,128)S(1)}, s32[8,3,1024]{2,1,0:T(4,128)}, ...), condition=%wide.region_2.3_spmd, body=%wide.region_0.2_spmd.sunk | while | flops 19935232 | bytes 21170268 | solution.py:67
  63.7 0.7 dynamic-slice_bitcast_fusion.2
  64.5 0.9 multiply_reduce_fusion.3
  65.4 0.7 rsqrt_multiply_fusion.2
  66.1 16.1 %multiply_convert_fusion.5 = (bf16[2,1024,512]{2,1,0:T(8,128)(2,1)S(1)}, bf16[2,1024,512]{2,1,0:T(8,128)(2,1)S(1)}) fusion(f32[1024,512]{1,0:T(8,128)S(1)} %get-tuple-element.158, f32[2]{0:T(128)S(1)} %bitcast.94, f32[1024,512]{1,0:T(8,128)S(1)} %get-tuple-element.159), kind=kLoop, calls=%fused_computation.2.clone.1 | loop fusion | flops 6291456 | bytes 8388616 | tf_op jit(solution)/shard_map/while/body/eval_jaxpr/convert_element_type | solution.py:33
  83.9 0.7 dynamic-slice_bitcast_fusion.2
  84.6 0.9 multiply_reduce_fusion.3
  85.5 0.7 rsqrt_multiply_fusion.2
  86.2 16.1 %multiply_convert_fusion.5 = (bf16[2,1024,512]{2,1,0:T(8,128)(2,1)S(1)}, bf16[2,1024,512]{2,1,0:T(8,128)(2,1)S(1)}) fusion(f32[1024,512]{1,0:T(8,128)S(1)} %get-tuple-element.158, f32[2]{0:T(128)S(1)} %bitcast.94, f32[1024,512]{1,0:T(8,128)S(1)} %get-tuple-element.159), kind=kLoop, calls=%fused_computation.2.clone.1 | loop fusion | flops 6291456 | bytes 8388616 | tf_op jit(solution)/shard_map/while/body/eval_jaxpr/convert_element_type | solution.py:33
  102.7 0.4 convolution_bitcast_fusion.11
  104.0 0.7 dynamic-slice_bitcast_fusion.2
  104.7 0.9 multiply_reduce_fusion.3
  105.7 0.7 rsqrt_multiply_fusion.2
  106.4 16.1 %multiply_convert_fusion.5 = (bf16[2,1024,512]{2,1,0:T(8,128)(2,1)S(1)}, bf16[2,1024,512]{2,1,0:T(8,128)(2,1)S(1)}) fusion(f32[1024,512]{1,0:T(8,128)S(1)} %get-tuple-element.158, f32[2]{0:T(128)S(1)} %bitcast.94, f32[1024,512]{1,0:T(8,128)S(1)} %get-tuple-element.159), kind=kLoop, calls=%fused_computation.2.clone.1 | loop fusion | flops 6291456 | bytes 8388616 | tf_op jit(solution)/shard_map/while/body/eval_jaxpr/convert_element_type | solution.py:33
  122.9 0.4 convolution_bitcast_fusion.11
  124.1 0.7 dynamic-slice_bitcast_fusion.2
  124.9 0.9 multiply_reduce_fusion.3
  125.8 0.7 rsqrt_multiply_fusion.2
  126.5 16.1 %multiply_convert_fusion.5 = (bf16[2,1024,512]{2,1,0:T(8,128)(2,1)S(1)}, bf16[2,1024,512]{2,1,0:T(8,128)(2,1)S(1)}) fusion(f32[1024,512]{1,0:T(8,128)S(1)} %get-tuple-element.158, f32[2]{0:T(128)S(1)} %bitcast.94, f32[1024,512]{1,0:T(8,128)S(1)} %get-tuple-element.159), kind=kLoop, calls=%fused_computation.2.clone.1 | loop fusion | flops 6291456 | bytes 8388616 | tf_op jit(solution)/shard_map/while/body/eval_jaxpr/convert_element_type | solution.py:33
  143.0 0.4 convolution_bitcast_fusion.11
  144.3 0.7 dynamic-slice_bitcast_fusion.2
  145.0 0.9 multiply_reduce_fusion.3
  145.9 0.7 rsqrt_multiply_fusion.2
  146.6 16.1 %multiply_convert_fusion.5 = (bf16[2,1024,512]{2,1,0:T(8,128)(2,1)S(1)}, bf16[2,1024,512]{2,1,0:T(8,128)(2,1)S(1)}) fusion(f32[1024,512]{1,0:T(8,128)S(1)} %get-tuple-element.158, f32[2]{0:T(128)S(1)} %bitcast.94, f32[1024,512]{1,0:T(8,128)S(1)} %get-tuple-element.159), kind=kLoop, calls=%fused_computation.2.clone.1 | loop fusion | flops 6291456 | bytes 8388616 | tf_op jit(solution)/shard_map/while/body/eval_jaxpr/convert_element_type | solution.py:33
  163.1 0.4 convolution_bitcast_fusion.11
  164.4 0.7 dynamic-slice_bitcast_fusion.2
  165.1 0.9 multiply_reduce_fusion.3
  166.1 0.7 rsqrt_multiply_fusion.2
  166.8 16.1 %multiply_convert_fusion.5 = (bf16[2,1024,512]{2,1,0:T(8,128)(2,1)S(1)}, bf16[2,1024,512]{2,1,0:T(8,128)(2,1)S(1)}) fusion(f32[1024,512]{1,0:T(8,128)S(1)} %get-tuple-element.158, f32[2]{0:T(128)S(1)} %bitcast.94, f32[1024,512]{1,0:T(8,128)S(1)} %get-tuple-element.159), kind=kLoop, calls=%fused_computation.2.clone.1 | loop fusion | flops 6291456 | bytes 8388616 | tf_op jit(solution)/shard_map/while/body/eval_jaxpr/convert_element_type | solution.py:33
  183.3 0.4 convolution_bitcast_fusion.11
  184.5 0.7 dynamic-slice_bitcast_fusion.2
  185.3 0.9 multiply_reduce_fusion.3
  186.2 0.7 rsqrt_multiply_fusion.2
  186.9 16.1 %multiply_convert_fusion.5 = (bf16[2,1024,512]{2,1,0:T(8,128)(2,1)S(1)}, bf16[2,1024,512]{2,1,0:T(8,128)(2,1)S(1)}) fusion(f32[1024,512]{1,0:T(8,128)S(1)} %get-tuple-element.158, f32[2]{0:T(128)S(1)} %bitcast.94, f32[1024,512]{1,0:T(8,128)S(1)} %get-tuple-element.159), kind=kLoop, calls=%fused_computation.2.clone.1 | loop fusion | flops 6291456 | bytes 8388616 | tf_op jit(solution)/shard_map/while/body/eval_jaxpr/convert_element_type | solution.py:33
  204.7 0.7 dynamic-slice_bitcast_fusion.2
  205.4 0.9 multiply_reduce_fusion.3
  206.4 0.7 rsqrt_multiply_fusion.2
  207.0 16.1 %multiply_convert_fusion.5 = (bf16[2,1024,512]{2,1,0:T(8,128)(2,1)S(1)}, bf16[2,1024,512]{2,1,0:T(8,128)(2,1)S(1)}) fusion(f32[1024,512]{1,0:T(8,128)S(1)} %get-tuple-element.158, f32[2]{0:T(128)S(1)} %bitcast.94, f32[1024,512]{1,0:T(8,128)S(1)} %get-tuple-element.159), kind=kLoop, calls=%fused_computation.2.clone.1 | loop fusion | flops 6291456 | bytes 8388616 | tf_op jit(solution)/shard_map/while/body/eval_jaxpr/convert_element_type | solution.py:33
  224.9 0.8 squeeze_reshape.3
  225.7 88.8 %all-reduce.2.cloned.1.call-done = f32[2,2,8192]{2,1,0:T(2,128)} async-done(((f32[2,2,8192]{2,1,0:T(2,128)}), f32[2,2,8192]{2,1,0:T(2,128)}) %all-reduce.2.cloned.1.call-update) | async-done | bytes 131088 | tf_op jit(solution)/shard_map/psum | solution.py:83
  314.4 0.7 multiply_reduce_fusion.1
  315.2 134.6 %psum.15 = f32[1024]{0:T(1024)S(1)} all-reduce(f32[1024]{0:T(1024)S(1)} %multiply_reduce_fusion.1), channel_id=1, replica_groups=mesh['tm'=64,'mic'=8] {'tm'}, use_global_device_ids=true, to_apply=%region_5.6 | all-reduce | flops 1024 | bytes 8192 | tf_op jit(solution)/shard_map/psum | solution.py:86
  449.8 0.6 broadcast_multiply_fusion
  (69 shorter events, 11.3 us)
Async XLA Ops:
  6.5 307.9 %all-reduce.2.cloned.1.call-start = ((), (), s32[]{:S(2)}) async-start(), calls=%async_computation | async-start | bytes 262144 | tf_op jit(solution)/shard_map/psum | solution.py:83
  6.5 52.5 %collective-permute-start = (bf16[4096,512]{1,0:T(8,128)(2,1)}, bf16[4096,512]{1,0:T(8,128)(2,1)}, u32[]{:S(2)}, u32[]{:S(2)}) collective-permute-start(bf16[4096,512]{1,0:T(8,128)(2,1)} %param.6), channel_id=1, source_target_pairs={{8,0},{16,8},{24,16},{32,24},{40,32},{48,40},{56,48},{64,56},{72,6... | collective-permute-start | bytes 12582920 | tf_op jit(solution)/shard_map/ppermute | solution.py:15
  18.3 45.5 %copy-start = (s32[3,512]{1,0:T(4,128)S(1)}, s32[3,512]{1,0:T(4,128)}, u32[]{:S(2)}) copy-start(s32[3,512]{1,0:T(4,128)} %param.7) | copy-start | bytes 18436
Sparse Core Ops, SparseCore 0:
  225.8 88.5 all-reduce.1
where the time goes:
time: 458 us; the launch traced here: 457 us
  other arithmetic  147 us (32%)
  blocking collectives  135 us (29%)
  waiting for transfers between devices  130 us (28%)
  matrix products  16.7 us (4%)
  between operations  13.5 us (3%)
  starting transfers between devices  8.78 us (2%)
  local copies, waits for them, and re-layouts  6.75 us (1%)
    psum x1, blocking collectives, local(): power_sum = lax.psum(local_power, 'tm')  135 us
    convert_element_type x8, other arithmetic, steer_block(): (strength[None] * jnp.cos(2.0 * math.pi * cycles)).astype(jnp.bfloat16)  129 us
    psum x1, waiting for transfers between devices, local(): summed = lax.psum(partial_value, 'mic')  88.8 us
    ppermute x1, waiting for transfers between devices, from_behind(): return lax.ppermute(shard, axis, pairs)  40.8 us
  transfers between devices with their start and end apart: 2, of which 2 were waited for; matrix products, arithmetic and copies ran while one was open for 1% of the time, Pallas kernels for 0%

commit v1 on v0

--- a/solution.py
+++ b/solution.py
@@ -83,7 +83,7 @@
     summed = lax.psum(partial_value, "mic")
     owned = lax.dynamic_slice_in_dim(summed, lax.axis_index("mic") * owned_count, owned_count, 2)
     local_power = jnp.sum(owned * owned, axis=(0, 1))
-    power_sum = lax.psum(local_power, "tm")
+    power_sum = jnp.sum(lax.all_gather(local_power, "tm"), axis=0)
     return power_sum / (spans * NBINS * MICS)
 
 

time: 458 us -> 407 us (0.89)
  blocking collectives: 135 us -> 83.5 us
    psum x1 -> x0, blocking collectives: 135 us -> none  [local(): power_sum = lax.psum(local_power, 'tm')]
    all_gather x0 -> x1, blocking collectives: none -> 83.5 us  [local(): power_sum = jnp.sum(lax.all_gather(local_power, 'tm'), axis=0)]
where the time goes in v1:
time: 407 us; the launch traced here: 406 us
  other arithmetic  147 us (36%)
  waiting for transfers between devices  130 us (32%)
  blocking collectives  83.5 us (21%)
  matrix products  16.7 us (4%)
  between operations  13.5 us (3%)
  starting transfers between devices  8.78 us (2%)
  local copies, waits for them, and re-layouts  6.79 us (2%)
    convert_element_type x8, other arithmetic, steer_block(): (strength[None] * jnp.cos(2.0 * math.pi * cycles)).astype(jnp.bfloat16)  129 us
    psum x1, waiting for transfers between devices, local(): summed = lax.psum(partial_value, 'mic')  88.8 us
    all_gather x1, blocking collectives, local(): power_sum = jnp.sum(lax.all_gather(local_power, 'tm'), axis=0)  83.5 us
    ppermute x1, waiting for transfers between devices, from_behind(): return lax.ppermute(shard, axis, pairs)  40.8 us
    ppermute x1, starting transfers between devices, from_behind(): return lax.ppermute(shard, axis, pairs)  8.78 us
  transfers between devices with their start and end apart: 2, of which 2 were waited for; matrix products, arithmetic and copies ran while one was open for 1% of the time, Pallas kernels for 0%

profile of v1, /device:TPU:1, one launch (start us, length us, event | category | flops | bytes accessed | tf_op | source)
XLA Modules:
  0.0 406.2 jit_solution(14925376594284844673)
XLA Ops:
  6.5 8.8 %collective-permute-start = (bf16[4096,512]{1,0:T(8,128)(2,1)}, bf16[4096,512]{1,0:T(8,128)(2,1)}, u32[]{:S(2)}, u32[]{:S(2)}) collective-permute-start(bf16[4096,512]{1,0:T(8,128)(2,1)} %param.6), channel_id=1, source_target_pairs={{8,0},{16,8},{24,16},{32,24},{40,32},{48,40},{56,48},{64,56},{72,6... | collective-permute-start | bytes 12582920 | tf_op jit(solution)/shard_map/ppermute | solution.py:15
  15.5 1.9 multiply_convert_fusion.3
  17.6 0.7 convert_bitcast_fusion
  18.3 40.8 %collective-permute-done = bf16[4096,512]{1,0:T(8,128)(2,1)} collective-permute-done((bf16[4096,512]{1,0:T(8,128)(2,1)}, bf16[4096,512]{1,0:T(8,128)(2,1)}, u32[]{:S(2)}, u32[]{:S(2)}) %collective-permute-start) | collective-permute-done | bytes 4194336 | tf_op jit(solution)/shard_map/ppermute | solution.py:15
  59.1 4.6 %fusion.16 = bf16[1,4,512]{2,1,0:T(4,128)(2,1)S(1)} fusion(bf16[4,8192]{1,0:T(4,128)(2,1)S(1)} %convert_element_type.74, bf16[4096,512]{1,0:T(8,128)(2,1)} %collective-permute-done, bf16[4096,512]{1,0:T(8,128)(2,1)} %param.6), kind=kOutput, calls=%fused_computation.36 | convolution fusion | flops 50333696 | bytes 8458240 | tf_op jit(solution)/shard_map/dot_general | solution.py:76
  63.7 161.1 %while.12 = (s32[]{:T(128)}, f32[8,1,2,2,1024]{4,3,2,1,0:T(2,128)S(1)}, s32[8,3,1024]{2,1,0:T(4,128)}, s32[3,512]{1,0:T(4,128)S(1)}, f32[2,1,1]{0,2,1:T(1,128)S(1)}, /*index=5*/bf16[1,4,512]{2,1,0:T(4,128)(2,1)S(1)}, s32[]{:T(128)}) while((s32[]{:T(128)}, f32[8,1,2,2,1024]{4,3,2,1,0:T(2,128)S(1)}, s32[8,3,1024]{2,1,0:T(4,128)}, ...), condition=%wide.region_2.3_spmd, body=%wide.region_0.2_spmd.sunk | while | flops 19935232 | bytes 21170268 | solution.py:67
  63.7 0.7 dynamic-slice_bitcast_fusion.2
  64.5 0.9 multiply_reduce_fusion.3
  65.4 0.7 rsqrt_multiply_fusion.2
  66.1 16.1 %multiply_convert_fusion.5 = (bf16[2,1024,512]{2,1,0:T(8,128)(2,1)S(1)}, bf16[2,1024,512]{2,1,0:T(8,128)(2,1)S(1)}) fusion(f32[1024,512]{1,0:T(8,128)S(1)} %get-tuple-element.158, f32[2]{0:T(128)S(1)} %bitcast.94, f32[1024,512]{1,0:T(8,128)S(1)} %get-tuple-element.159), kind=kLoop, calls=%fused_computation.2.clone.1 | loop fusion | flops 6291456 | bytes 8388616 | tf_op jit(solution)/shard_map/while/body/eval_jaxpr/convert_element_type | solution.py:33
  83.9 0.7 dynamic-slice_bitcast_fusion.2
  84.6 0.9 multiply_reduce_fusion.3
  85.5 0.7 rsqrt_multiply_fusion.2
  86.2 16.1 %multiply_convert_fusion.5 = (bf16[2,1024,512]{2,1,0:T(8,128)(2,1)S(1)}, bf16[2,1024,512]{2,1,0:T(8,128)(2,1)S(1)}) fusion(f32[1024,512]{1,0:T(8,128)S(1)} %get-tuple-element.158, f32[2]{0:T(128)S(1)} %bitcast.94, f32[1024,512]{1,0:T(8,128)S(1)} %get-tuple-element.159), kind=kLoop, calls=%fused_computation.2.clone.1 | loop fusion | flops 6291456 | bytes 8388616 | tf_op jit(solution)/shard_map/while/body/eval_jaxpr/convert_element_type | solution.py:33
  102.7 0.4 convolution_bitcast_fusion.11
  104.0 0.7 dynamic-slice_bitcast_fusion.2
  104.7 0.9 multiply_reduce_fusion.3
  105.7 0.7 rsqrt_multiply_fusion.2
  106.4 16.1 %multiply_convert_fusion.5 = (bf16[2,1024,512]{2,1,0:T(8,128)(2,1)S(1)}, bf16[2,1024,512]{2,1,0:T(8,128)(2,1)S(1)}) fusion(f32[1024,512]{1,0:T(8,128)S(1)} %get-tuple-element.158, f32[2]{0:T(128)S(1)} %bitcast.94, f32[1024,512]{1,0:T(8,128)S(1)} %get-tuple-element.159), kind=kLoop, calls=%fused_computation.2.clone.1 | loop fusion | flops 6291456 | bytes 8388616 | tf_op jit(solution)/shard_map/while/body/eval_jaxpr/convert_element_type | solution.py:33
  122.9 0.4 convolution_bitcast_fusion.11
  124.1 0.7 dynamic-slice_bitcast_fusion.2
  124.9 0.9 multiply_reduce_fusion.3
  125.8 0.7 rsqrt_multiply_fusion.2
  126.5 16.1 %multiply_convert_fusion.5 = (bf16[2,1024,512]{2,1,0:T(8,128)(2,1)S(1)}, bf16[2,1024,512]{2,1,0:T(8,128)(2,1)S(1)}) fusion(f32[1024,512]{1,0:T(8,128)S(1)} %get-tuple-element.158, f32[2]{0:T(128)S(1)} %bitcast.94, f32[1024,512]{1,0:T(8,128)S(1)} %get-tuple-element.159), kind=kLoop, calls=%fused_computation.2.clone.1 | loop fusion | flops 6291456 | bytes 8388616 | tf_op jit(solution)/shard_map/while/body/eval_jaxpr/convert_element_type | solution.py:33
  143.0 0.4 convolution_bitcast_fusion.11
  144.3 0.7 dynamic-slice_bitcast_fusion.2
  145.0 0.9 multiply_reduce_fusion.3
  145.9 0.7 rsqrt_multiply_fusion.2
  146.6 16.1 %multiply_convert_fusion.5 = (bf16[2,1024,512]{2,1,0:T(8,128)(2,1)S(1)}, bf16[2,1024,512]{2,1,0:T(8,128)(2,1)S(1)}) fusion(f32[1024,512]{1,0:T(8,128)S(1)} %get-tuple-element.158, f32[2]{0:T(128)S(1)} %bitcast.94, f32[1024,512]{1,0:T(8,128)S(1)} %get-tuple-element.159), kind=kLoop, calls=%fused_computation.2.clone.1 | loop fusion | flops 6291456 | bytes 8388616 | tf_op jit(solution)/shard_map/while/body/eval_jaxpr/convert_element_type | solution.py:33
  163.1 0.4 convolution_bitcast_fusion.11
  164.4 0.7 dynamic-slice_bitcast_fusion.2
  165.1 0.9 multiply_reduce_fusion.3
  166.1 0.7 rsqrt_multiply_fusion.2
  166.8 16.1 %multiply_convert_fusion.5 = (bf16[2,1024,512]{2,1,0:T(8,128)(2,1)S(1)}, bf16[2,1024,512]{2,1,0:T(8,128)(2,1)S(1)}) fusion(f32[1024,512]{1,0:T(8,128)S(1)} %get-tuple-element.158, f32[2]{0:T(128)S(1)} %bitcast.94, f32[1024,512]{1,0:T(8,128)S(1)} %get-tuple-element.159), kind=kLoop, calls=%fused_computation.2.clone.1 | loop fusion | flops 6291456 | bytes 8388616 | tf_op jit(solution)/shard_map/while/body/eval_jaxpr/convert_element_type | solution.py:33
  183.3 0.4 convolution_bitcast_fusion.11
  184.5 0.7 dynamic-slice_bitcast_fusion.2
  185.3 0.9 multiply_reduce_fusion.3
  186.2 0.7 rsqrt_multiply_fusion.2
  186.9 16.1 %multiply_convert_fusion.5 = (bf16[2,1024,512]{2,1,0:T(8,128)(2,1)S(1)}, bf16[2,1024,512]{2,1,0:T(8,128)(2,1)S(1)}) fusion(f32[1024,512]{1,0:T(8,128)S(1)} %get-tuple-element.158, f32[2]{0:T(128)S(1)} %bitcast.94, f32[1024,512]{1,0:T(8,128)S(1)} %get-tuple-element.159), kind=kLoop, calls=%fused_computation.2.clone.1 | loop fusion | flops 6291456 | bytes 8388616 | tf_op jit(solution)/shard_map/while/body/eval_jaxpr/convert_element_type | solution.py:33
  204.7 0.7 dynamic-slice_bitcast_fusion.2
  205.4 0.9 multiply_reduce_fusion.3
  206.4 0.7 rsqrt_multiply_fusion.2
  207.0 16.1 %multiply_convert_fusion.5 = (bf16[2,1024,512]{2,1,0:T(8,128)(2,1)S(1)}, bf16[2,1024,512]{2,1,0:T(8,128)(2,1)S(1)}) fusion(f32[1024,512]{1,0:T(8,128)S(1)} %get-tuple-element.158, f32[2]{0:T(128)S(1)} %bitcast.94, f32[1024,512]{1,0:T(8,128)S(1)} %get-tuple-element.159), kind=kLoop, calls=%fused_computation.2.clone.1 | loop fusion | flops 6291456 | bytes 8388616 | tf_op jit(solution)/shard_map/while/body/eval_jaxpr/convert_element_type | solution.py:33
  224.9 0.8 squeeze_reshape.3
  225.7 88.8 %all-reduce.2.cloned.1.call-done = f32[2,2,8192]{2,1,0:T(2,128)} async-done(((f32[2,2,8192]{2,1,0:T(2,128)}), f32[2,2,8192]{2,1,0:T(2,128)}) %all-reduce.2.cloned.1.call-update) | async-done | bytes 131088 | tf_op jit(solution)/shard_map/psum | solution.py:83
  314.4 0.7 multiply_reduce_fusion.1
  315.2 83.5 %all-gather = f32[65536]{0:T(1024)S(1)} all-gather(f32[1024]{0:T(1024)S(1)} %multiply_reduce_fusion.1), channel_id=2, replica_groups=mesh['tm'=64,'mic'=8] {'tm'}, dimensions={0}, use_global_device_ids=true | all-gather | bytes 266240 | tf_op jit(solution)/shard_map/all_gather | solution.py:86
  398.8 0.6 broadcast_multiply_fusion
  (71 shorter events, 11.3 us)
Async XLA Ops:
  6.5 307.9 %all-reduce.2.cloned.1.call-start = ((), (), s32[]{:S(2)}) async-start(), calls=%async_computation | async-start | bytes 262144 | tf_op jit(solution)/shard_map/psum | solution.py:83
  6.5 52.5 %collective-permute-start = (bf16[4096,512]{1,0:T(8,128)(2,1)}, bf16[4096,512]{1,0:T(8,128)(2,1)}, u32[]{:S(2)}, u32[]{:S(2)}) collective-permute-start(bf16[4096,512]{1,0:T(8,128)(2,1)} %param.6), channel_id=1, source_target_pairs={{8,0},{16,8},{24,16},{32,24},{40,32},{48,40},{56,48},{64,56},{72,6... | collective-permute-start | bytes 12582920 | tf_op jit(solution)/shard_map/ppermute | solution.py:15
  18.3 45.5 %copy-start = (s32[3,512]{1,0:T(4,128)S(1)}, s32[3,512]{1,0:T(4,128)}, u32[]{:S(2)}) copy-start(s32[3,512]{1,0:T(4,128)} %param.7) | copy-start | bytes 18436
Sparse Core Ops, SparseCore 0:
  225.8 88.5 all-reduce.1
